TPU v7x, 128 devices: a whole 4x4x4 slice. The times are simulated.
128 devices in a mesh: section: 2 (over x_hi), pair: 2 (over x_lo), dp: 32 (over z, y, core).
Axes of the slice: x: 4 (x_hi: 2, x_lo: 2; x = x_hi * 2 + x_lo), y: 4, z: 4, core: 2. Of those that a mesh axis runs over, the one named last changes fastest.
Arguments:
- tokens: bfloat16 [2, 64, 128, 1280], P(None, ('pair', 'dp')), may hold values from -6 to 6
- lengths: int32 [2, 64], P(None, ('pair', 'dp')), may hold values from 32 to 128, as said below
- cotangent: bfloat16 [2, 64, 128, 1280], P(None, ('pair', 'dp')), may hold values from -6 to 6
- w_qkv: bfloat16 [2, 1280, 3840], P('section', 'pair'), may hold values from -0.15625 to 0.15625
- w_out: bfloat16 [2, 1280, 1280], P('section', 'pair'), may hold values from -0.625 to 0.625
- w_up: bfloat16 [2, 1280, 5120], P('section', 'pair'), may hold values from -0.15625 to 0.15625
- w_down: bfloat16 [2, 5120, 1280], P('section', 'pair'), may hold values from -0.078125 to 0.078125
- norm1_gain: float32 [2, 1280], P('section'), may hold values from 0.5 to 1.5
- norm1_bias: float32 [2, 1280], P('section'), may hold values from -3 to 3
- norm2_gain: float32 [2, 1280], P('section'), may hold values from 0.5 to 1.5
- norm2_bias: float32 [2, 1280], P('section'), may hold values from -3 to 3
Outputs:
- layer_outputs: bfloat16 [2, 2, 64, 128, 1280], P('section', None, ('pair', 'dp'))
- input_grads: bfloat16 [2, 2, 64, 128, 1280], P('section', None, ('pair', 'dp'))
- grad_qkv: float32 [2, 1280, 3840], P('section', ('pair', 'dp'))
- grad_out: float32 [2, 1280, 1280], P('section', ('pair', 'dp'))
- grad_up: float32 [2, 1280, 5120], P('section', ('pair', 'dp'))
- grad_down: float32 [2, 5120, 1280], P('section', ('pair', 'dp'))
- grad_norm1_gain: float32 [2, 1280], P('section', ('pair', 'dp'))
- grad_norm1_bias: float32 [2, 1280], P('section', ('pair', 'dp'))
- grad_norm2_gain: float32 [2, 1280], P('section', ('pair', 'dp'))
- grad_norm2_bias: float32 [2, 1280], P('section', ('pair', 'dp'))
Inputs may be any that keep to these rules, and one draw needn't show every extreme that they name: `lengths`: in every micro-batch one sentence has length 128 and another 128 // 4.
All inputs are finite; a program needn't handle non-finite values.
Results may differ from a plain program's by a relative error of at most 0.017.
Values may be sent and summed in bfloat16 or wider, within the bound.
No kernel may reach another device: no remote copies, remote signals or barrier semaphores. Data moves between devices by JAX's collectives and lax.ppermute only.
A program may use at most 832 MiB of HBM per device.

v0:
```python
import jax
import jax.numpy as jnp
from jax import lax
from jax.sharding import PartitionSpec as P

HEADS = 20


EPSILON = 1e-05


def passed_along(value, axis, steps):
    count = lax.axis_size(axis)
    initial, last = (max(0, -steps), min(count, count - steps))
    return lax.ppermute(value, axis, [(source, source + steps) for source in range(initial, last)])


def send_forward(result_low):
    return passed_along(result_low, "section", 1)


def send_backward(grad_low):
    return passed_along(grad_low, "section", -1)


def normalize(values, gain_row, bias_row):
    row_mean = jnp.mean(values, axis=-1, keepdims=True)
    centred = values - row_mean
    variance = jnp.mean(centred * centred, axis=-1, keepdims=True)
    inv_std = lax.rsqrt(variance + EPSILON)
    x_hat = centred * inv_std
    return (x_hat * gain_row + bias_row, x_hat, inv_std)


def norm_back(grad_rows, x_hat, inv_std, gain_row):
    scaled = grad_rows * gain_row
    first_mean = jnp.mean(scaled, axis=-1, keepdims=True)
    second_mean = jnp.mean(scaled * x_hat, axis=-1, keepdims=True)
    return inv_std * (scaled - first_mean - x_hat * second_mean)


def gelu_exact(values):
    return jax.nn.gelu(values, approximate=False)


def split_heads(qkv_low, model_width):
    seq_len = qkv_low.shape[0]
    head_dim = model_width // HEADS
    query_h = qkv_low[:, :model_width].reshape(seq_len, HEADS, head_dim)
    key_h = qkv_low[:, model_width : 2 * model_width].reshape(seq_len, HEADS, head_dim)
    value_h = qkv_low[:, 2 * model_width :].reshape(seq_len, HEADS, head_dim)
    return (query_h, key_h, value_h)


def layer_forward(weights, norm_params, x_low, keys_valid):
    w_qkv, w_out, w_up, w_down = weights
    gain_one, bias_one, gain_two, bias_two = norm_params
    seq_len, model_width = x_low.shape
    score_scale = (model_width // HEADS) ** (-0.5)
    x_full = x_low.astype(jnp.float32)
    normed, _, _ = normalize(x_full, gain_one, bias_one)
    qkv_low = jnp.dot(
        normed.astype(jnp.bfloat16), w_qkv, preferred_element_type=jnp.float32
    ).astype(jnp.bfloat16)
    query_h, key_h, value_h = split_heads(qkv_low, model_width)
    scores = (
        jnp.einsum("qhd,khd->hqk", query_h, key_h, preferred_element_type=jnp.float32) * score_scale
    )
    scores = jnp.where(keys_valid[None, None, :], scores, -1e30)
    row_top = jnp.max(scores, axis=-1, keepdims=True)
    raised = jnp.exp(scores - row_top)
    totals = jnp.sum(raised, axis=-1, keepdims=True)
    attention = raised / totals
    log_total = (row_top + jnp.log(totals))[..., 0]
    mixed_low = jnp.einsum(
        "hqk,khd->qhd", attention.astype(jnp.bfloat16), value_h, preferred_element_type=jnp.float32
    )
    mixed_low = mixed_low.reshape(seq_len, model_width).astype(jnp.bfloat16)
    middle = x_full + jnp.dot(mixed_low, w_out, preferred_element_type=jnp.float32)
    normed_two, _, _ = normalize(middle, gain_two, bias_two)
    hidden = jnp.dot(normed_two.astype(jnp.bfloat16), w_up, preferred_element_type=jnp.float32)
    active = gelu_exact(hidden).astype(jnp.bfloat16)
    output = middle + jnp.dot(active, w_down, preferred_element_type=jnp.float32)
    return (output, (x_low, qkv_low, log_total, mixed_low, middle, hidden))


def layer_backward(weights, norm_params, kept_values, grad_rows, keys_valid):
    w_qkv, w_out, w_up, w_down = weights
    gain_one, bias_one, gain_two, bias_two = norm_params
    x_low, qkv_low, log_total, mixed_low, middle, hidden = kept_values
    seq_len, model_width = x_low.shape
    head_dim = model_width // HEADS
    score_scale = head_dim ** (-0.5)
    grad_low = grad_rows.astype(jnp.bfloat16)
    active = gelu_exact(hidden).astype(jnp.bfloat16)
    grad_down = jnp.dot(active.T, grad_low, preferred_element_type=jnp.float32)
    grad_active = jnp.dot(grad_low, w_down.T, preferred_element_type=jnp.float32)
    _, gelu_pull = jax.vjp(gelu_exact, hidden)
    grad_hidden = gelu_pull(grad_active)[0].astype(jnp.bfloat16)
    normed_two, hat_two, inv_two = normalize(middle, gain_two, bias_two)
    grad_up = jnp.dot(
        normed_two.astype(jnp.bfloat16).T, grad_hidden, preferred_element_type=jnp.float32
    )
    grad_normed_two = jnp.dot(grad_hidden, w_up.T, preferred_element_type=jnp.float32)
    grad_gain_two = jnp.sum(grad_normed_two * hat_two, axis=0)
    grad_bias_two = jnp.sum(grad_normed_two, axis=0)
    grad_middle = grad_rows + norm_back(grad_normed_two, hat_two, inv_two, gain_two)
    middle_low = grad_middle.astype(jnp.bfloat16)
    grad_out = jnp.dot(mixed_low.T, middle_low, preferred_element_type=jnp.float32)
    grad_mixed = jnp.dot(middle_low, w_out.T, preferred_element_type=jnp.float32).astype(
        jnp.bfloat16
    )
    grad_mixed = grad_mixed.reshape(seq_len, HEADS, head_dim)
    query_h, key_h, value_h = split_heads(qkv_low, model_width)
    scores = (
        jnp.einsum("qhd,khd->hqk", query_h, key_h, preferred_element_type=jnp.float32) * score_scale
    )
    scores = jnp.where(keys_valid[None, None, :], scores, -1e30)
    attention = jnp.exp(scores - log_total[..., None])
    grad_value = jnp.einsum(
        "hqk,qhd->khd",
        attention.astype(jnp.bfloat16),
        grad_mixed,
        preferred_element_type=jnp.float32,
    )
    grad_attention = jnp.einsum(
        "qhd,khd->hqk", grad_mixed, value_h, preferred_element_type=jnp.float32
    )
    row_inner = jnp.sum(grad_attention * attention, axis=-1, keepdims=True)
    grad_scores = (attention * (grad_attention - row_inner)).astype(jnp.bfloat16)
    grad_query = (
        jnp.einsum("hqk,khd->qhd", grad_scores, key_h, preferred_element_type=jnp.float32)
        * score_scale
    )
    grad_key = (
        jnp.einsum("hqk,qhd->khd", grad_scores, query_h, preferred_element_type=jnp.float32)
        * score_scale
    )
    grad_qkv_low = jnp.concatenate(
        [
            grad_query.reshape(seq_len, model_width),
            grad_key.reshape(seq_len, model_width),
            grad_value.reshape(seq_len, model_width),
        ],
        axis=1,
    ).astype(jnp.bfloat16)
    x_full = x_low.astype(jnp.float32)
    normed_one, hat_one, inv_one = normalize(x_full, gain_one, bias_one)
    grad_qkv = jnp.dot(
        normed_one.astype(jnp.bfloat16).T, grad_qkv_low, preferred_element_type=jnp.float32
    )
    grad_normed_one = jnp.dot(grad_qkv_low, w_qkv.T, preferred_element_type=jnp.float32)
    grad_gain_one = jnp.sum(grad_normed_one * hat_one, axis=0)
    grad_bias_one = jnp.sum(grad_normed_one, axis=0)
    grad_inputs = grad_middle + norm_back(grad_normed_one, hat_one, inv_one, gain_one)
    return (
        grad_inputs,
        (
            grad_qkv,
            grad_out,
            grad_up,
            grad_down,
            grad_gain_one,
            grad_bias_one,
            grad_gain_two,
            grad_bias_two,
        ),
    )


def store_slot(stored, update, slot_index, active_flag):
    current = lax.dynamic_index_in_dim(stored, slot_index, 0, keepdims=False)
    return lax.dynamic_update_index_in_dim(
        stored, jnp.where(active_flag, update, current), slot_index, 0
    )


def kept_zeros(seq_len, model_width, hidden_width):
    return (
        jnp.zeros((seq_len, model_width), jnp.bfloat16),
        jnp.zeros((seq_len, 3 * model_width), jnp.bfloat16),
        jnp.zeros((HEADS, seq_len), jnp.float32),
        jnp.zeros((seq_len, model_width), jnp.bfloat16),
        jnp.zeros((seq_len, model_width), jnp.float32),
        jnp.zeros((seq_len, hidden_width), jnp.float32),
    )


def shards(
    tokens,
    lengths,
    cotangent,
    w_qkv,
    w_out,
    w_up,
    w_down,
    norm1_gain,
    norm1_bias,
    norm2_gain,
    norm2_bias,
):
    micro_count = tokens.shape[0]
    seq_len = tokens.shape[2]
    model_width = tokens.shape[3]
    section_index = lax.axis_index("section")
    norm_params = (norm1_gain[0], norm1_bias[0], norm2_gain[0], norm2_bias[0])
    positions = jnp.arange(seq_len, dtype=jnp.int32)
    own_lengths = lengths[:, 0]
    outputs_buffer = jnp.zeros((micro_count, seq_len, model_width), jnp.bfloat16)
    inputs_buffer = jnp.zeros((micro_count, seq_len, model_width), jnp.bfloat16)
    full_qkv, full_out, full_up, full_down = (
        lax.all_gather(w_qkv, "pair", axis=1, tiled=True),
        lax.all_gather(w_out, "pair", axis=1, tiled=True),
        lax.all_gather(w_up, "pair", axis=1, tiled=True),
        lax.all_gather(w_down, "pair", axis=1, tiled=True),
    )
    weights = (full_qkv[0], full_out[0], full_up[0], full_down[0])
    hidden_width = weights[2].shape[1]

    def run_forward(x_low, keys_valid):
        return layer_forward(weights, norm_params, x_low, keys_valid)

    def skip_forward(x_low, keys_valid):
        return (
            jnp.zeros((seq_len, model_width), jnp.float32),
            kept_zeros(seq_len, model_width, hidden_width),
        )

    def run_backward(kept_values, grad_rows, keys_valid):
        return layer_backward(weights, norm_params, kept_values, grad_rows, keys_valid)

    def skip_backward(kept_values, grad_rows, keys_valid):
        zero_grads = tuple(
            (jnp.zeros(tensor.shape, jnp.float32) for tensor in weights + norm_params)
        )
        return (jnp.zeros((seq_len, model_width), jnp.float32), zero_grads)

    first_kept = kept_zeros(seq_len, model_width, hidden_width)
    kept_buffer = jax.tree.map(
        lambda leaf_value: jnp.zeros((micro_count,) + leaf_value.shape, leaf_value.dtype),
        first_kept,
    )
    arriving = jnp.zeros((seq_len, model_width), jnp.bfloat16)
    for step_count in range(micro_count + 1):
        position = step_count - section_index
        active_flag = (position >= 0) & (position < micro_count)
        slot_index = jnp.clip(position, 0, micro_count - 1)
        keys_valid = positions < lax.dynamic_index_in_dim(
            own_lengths, slot_index, 0, keepdims=False
        )
        x_low = jnp.where(section_index == 0, tokens[min(step_count, micro_count - 1), 0], arriving)
        result, kept_values = lax.cond(active_flag, run_forward, skip_forward, x_low, keys_valid)
        result_low = result.astype(jnp.bfloat16)
        outputs_buffer = store_slot(outputs_buffer, result_low, slot_index, active_flag)
        kept_buffer = jax.tree.map(
            lambda stored, update: store_slot(stored, update, slot_index, active_flag),
            kept_buffer,
            kept_values,
        )
        if step_count < micro_count:
            arriving = send_forward(result_low)
    grads_total = tuple((jnp.zeros(tensor.shape, jnp.float32) for tensor in weights + norm_params))
    arriving = jnp.zeros((seq_len, model_width), jnp.bfloat16)
    for step_count in range(micro_count + 1):
        position = step_count - 1 + section_index
        active_flag = (position >= 0) & (position < micro_count)
        slot_index = jnp.clip(position, 0, micro_count - 1)
        keys_valid = positions < lax.dynamic_index_in_dim(
            own_lengths, slot_index, 0, keepdims=False
        )
        kept_values = jax.tree.map(
            lambda stored: lax.dynamic_index_in_dim(stored, slot_index, 0, keepdims=False),
            kept_buffer,
        )
        grad_rows = jnp.where(
            section_index == 1, cotangent[min(step_count, micro_count - 1), 0], arriving
        ).astype(jnp.float32)
        grad_inputs, layer_grads = lax.cond(
            active_flag, run_backward, skip_backward, kept_values, grad_rows, keys_valid
        )
        grad_low = grad_inputs.astype(jnp.bfloat16)
        inputs_buffer = store_slot(inputs_buffer, grad_low, slot_index, active_flag)
        grads_total = tuple(
            (total_part + new_part for total_part, new_part in zip(grads_total, layer_grads))
        )
        if step_count < micro_count:
            arriving = send_backward(grad_low)
    stacked = tuple((tensor[None] for tensor in grads_total))
    summed = (
        lax.psum_scatter(stacked[0], ("pair", "dp"), scatter_dimension=1, tiled=True),
        lax.psum_scatter(stacked[1], ("pair", "dp"), scatter_dimension=1, tiled=True),
        lax.psum_scatter(stacked[2], ("pair", "dp"), scatter_dimension=1, tiled=True),
        lax.psum_scatter(stacked[3], ("pair", "dp"), scatter_dimension=1, tiled=True),
        lax.psum_scatter(stacked[4], ("pair", "dp"), scatter_dimension=1, tiled=True),
        lax.psum_scatter(stacked[5], ("pair", "dp"), scatter_dimension=1, tiled=True),
        lax.psum_scatter(stacked[6], ("pair", "dp"), scatter_dimension=1, tiled=True),
        lax.psum_scatter(stacked[7], ("pair", "dp"), scatter_dimension=1, tiled=True),
    )
    layer_outputs = outputs_buffer[None, :, None]
    input_grads = inputs_buffer[None, :, None]
    return (
        layer_outputs,
        input_grads,
        summed[0],
        summed[1],
        summed[2],
        summed[3],
        summed[4],
        summed[5],
        summed[6],
        summed[7],
    )


def solution(mesh):
    in_specs = (
        P(None, ("pair", "dp"), None, None),
        P(None, ("pair", "dp")),
        P(None, ("pair", "dp"), None, None),
        P("section", "pair", None),
        P("section", "pair", None),
        P("section", "pair", None),
        P("section", "pair", None),
        P("section", None),
        P("section", None),
        P("section", None),
        P("section", None),
    )
    out_specs = (
        P("section", None, ("pair", "dp"), None, None),
        P("section", None, ("pair", "dp"), None, None),
        P("section", ("pair", "dp"), None),
        P("section", ("pair", "dp"), None),
        P("section", ("pair", "dp"), None),
        P("section", ("pair", "dp"), None),
        P("section", ("pair", "dp")),
        P("section", ("pair", "dp")),
        P("section", ("pair", "dp")),
        P("section", ("pair", "dp")),
    )
    return jax.shard_map(shards, mesh=mesh, in_specs=in_specs, out_specs=out_specs, check_vma=False)
```

profile of v0, /device:TPU:0, one launch (start us, length us, event | category | flops | bytes accessed | tf_op | source)
XLA Modules:
  0.0 3101.6 jit_solution(3713549697215760923)
XLA Ops:
  10.5 50.6 %all-gather.7.cloned.1.call-done = bf16[1,1280,1280]{2,1,0:T(8,128)(2,1)} async-done(((bf16[1,640,1280]{2,1,0:T(8,128)(2,1)}), bf16[1,1280,1280]{2,1,0:T(8,128)(2,1)}) %all-gather.7.cloned.1.call-update) | async-done | bytes 3276816 | tf_op jit(solution)/shard_map/all_gather | solution.py:213
  61.1 127.5 %all-gather.5.cloned.1.call-done = bf16[1,1280,3840]{2,1,0:T(8,128)(2,1)} async-done(((bf16[1,640,3840]{2,1,0:T(8,128)(2,1)}), bf16[1,1280,3840]{2,1,0:T(8,128)(2,1)}) %all-gather.5.cloned.1.call-update) | async-done | bytes 9830416 | tf_op jit(solution)/shard_map/all_gather | solution.py:212
  188.6 163.5 %all-gather.9.cloned.1.call-done = bf16[1,1280,5120]{2,1,0:T(8,128)(2,1)} async-done(((bf16[1,640,5120]{2,1,0:T(8,128)(2,1)}), bf16[1,1280,5120]{2,1,0:T(8,128)(2,1)}) %all-gather.9.cloned.1.call-update) | async-done | bytes 13107216 | tf_op jit(solution)/shard_map/all_gather | solution.py:214
  352.0 163.3 %all-gather.11.cloned.1.call-done = bf16[1,5120,1280]{2,1,0:T(8,128)(2,1)} async-done(((bf16[1,2560,1280]{2,1,0:T(8,128)(2,1)}), bf16[1,5120,1280]{2,1,0:T(8,128)(2,1)}) %all-gather.11.cloned.1.call-update) | async-done | bytes 13107216 | tf_op jit(solution)/shard_map/all_gather | solution.py:215
  515.5 37.4 %conditional.6 = (bf16[128,1280]{1,0:T(8,128)(2,1)S(1)}, f32[20,128]{1,0:T(8,128)S(1)}, f32[128,1280]{1,0:T(8,128)S(1)}, f32[128,5120]{1,0:T(8,128)}, bf16[128,1...) conditional(s32[]{:T(128)} %convert_element_type.345, () %tuple.86, ...), branch_computations={%region_0.1_spmd, %region_1.8_spmd} | conditional | flops 5167183872 | bytes 83875816 | solution.py:252
  539.2 11.5 fusion.10
  570.5 40.9 %conditional.7 = (bf16[128,1280]{1,0:T(8,128)(2,1)S(1)}, f32[20,128]{1,0:T(8,128)S(1)}, f32[128,1280]{1,0:T(8,128)S(1)}, f32[128,5120]{1,0:T(8,128)}, bf16[128,1...) conditional(s32[]{:T(128)} %convert_element_type.346, () %tuple.88, ...), branch_computations={%region_8.9_spmd, %region_9.16_spmd} | conditional | flops 5167183872 | bytes 94361664 | solution.py:252
  595.3 11.8 fusion.100
  643.0 38.1 %conditional.9 = (f32[1280,3840]{1,0:T(8,128)}, f32[1280,1280]{1,0:T(8,128)}, f32[1280,5120]{1,0:T(8,128)}, f32[5120,1280]{1,0:T(8,128)}, f32[1280]{0:T(1024)S(1...) conditional(s32[]{:T(128)} %convert_element_type.348, () %tuple.92, ...), branch_computations={%region_24.25_spmd, %region_25.39_spmd} | conditional | flops 10386137088 | bytes 186641440 | solution.py:278
  643.0 12.0 broadcast.1294
  655.0 10.3 broadcast.1295
  682.4 81.7 %collective-permute-done.2 = bf16[128,1280]{1,0:T(8,128)(2,1)S(1)} collective-permute-done((bf16[128,1280]{1,0:T(8,128)(2,1)}, bf16[128,1280]{1,0:T(8,128)(2,1)S(1)}, u32[]{:S(2)}, u32[]{:S(2)}) %collective-permute-start.2) | collective-permute-done | bytes 327712 | tf_op jit(solution)/shard_map/ppermute | solution.py:15
  766.0 80.7 %conditional.10 = (f32[1280,3840]{1,0:T(8,128)}, f32[1280,1280]{1,0:T(8,128)}, f32[1280,5120]{1,0:T(8,128)}, f32[5120,1280]{1,0:T(8,128)}, f32[1280]{0:T(1024)S(...) conditional(s32[]{:T(128)} %convert_element_type.351, () %tuple.94, ...), branch_computations={%region_39.40_spmd, %region_40.54_spmd} | conditional | flops 10385809408 | bytes 187621920 | solution.py:278
  766.4 12.9 fusion.355
  815.8 12.2 fusion.397
  831.7 15.1 fusion.372
  848.1 10.6 collective-permute-done.3
  860.6 81.4 %conditional.11 = (f32[1280,3840]{1,0:T(8,128)}, f32[1280,1280]{1,0:T(8,128)}, f32[1280,5120]{1,0:T(8,128)}, f32[5120,1280]{1,0:T(8,128)}, f32[1280]{0:T(1024)S(...) conditional(s32[]{:T(128)} %convert_element_type.353, () %tuple.96, ...), branch_computations={%region_54.55_spmd, %region_55.69_spmd} | conditional | flops 10385809408 | bytes 187621920 | solution.py:278
  861.4 12.8 fusion.431
  910.8 12.2 fusion.473
  926.6 15.1 fusion.448
  942.0 10.6 add_add_fusion.2
  962.5 26.3 add_add_fusion.1
  988.8 23.0 broadcast_in_dim.273
  1011.8 34.7 %add_add_fusion = f32[1280,5120]{1,0:T(8,128)} fusion(f32[1280,5120]{1,0:T(8,128)} %get-tuple-element.833, f32[1280,5120]{1,0:T(8,128)} %get-tuple-element.831, f32[1280,5120]{1,0:T(8,128)} %get-tuple-element.832), kind=kLoop, calls=%fused_computation.677 | loop fusion | flops 13107200 | bytes 104857600 | tf_op jit(solution)/shard_map/add | solution.py:284
  1046.5 21.6 broadcast_in_dim.275
  1068.2 34.4 %add_bitcast_fusion = f32[1,5120,1280]{2,1,0:T(8,128)} fusion(f32[5120,1280]{1,0:T(8,128)} %get-tuple-element.836, f32[5120,1280]{1,0:T(8,128)} %get-tuple-element.834, f32[5120,1280]{1,0:T(8,128)} %get-tuple-element.835), kind=kLoop, calls=%fused_computation.676 | loop fusion | flops 13107200 | bytes 104857600 | tf_op jit(solution)/shard_map/broadcast_in_dim | solution.py:288
  1108.7 277.2 %all-reduce.7 = (f32[1,1280]{1,0:T(1,128)S(1)}, f32[1,1280]{1,0:T(1,128)S(1)}, f32[1,1280]{1,0:T(1,128)S(1)}, f32[1,1280]{1,0:T(1,128)S(1)}) all-reduce(f32[1,1280]{1,0:T(1,128)S(1)} %broadcast_in_dim.277, f32[1,1280]{1,0:T(1,128)S(1)} %broadcast_in_dim.278, ...), channel_id=6, replica_groups=mesh['section'=2,'pair'=2,'dp'=32] {'pair','dp'}, use_global_device_ids=true, to_apply=%region_73.74.clone | all-reduce | flops 5120 | bytes 40960
  1389.3 138.1 %all-reduce.14.cloned.1.call-done = f32[1,1280,1280]{2,0,1:T(1,128)} async-done(((f32[1,1280,1280]{2,0,1:T(1,128)}), f32[1,1280,1280]{2,0,1:T(1,128)}) %all-reduce.14.cloned.1.call-update) | async-done | bytes 6553616
  1529.0 604.8 %all-reduce.12.cloned.1.call-done = f32[1,1280,3840]{2,0,1:T(1,128)} async-done(((f32[1,1280,3840]{2,0,1:T(1,128)}), f32[1,1280,3840]{2,0,1:T(1,128)}) %all-reduce.12.cloned.1.call-update) | async-done | bytes 19660816
  2135.6 626.3 %all-reduce.16.cloned.1.call-done = f32[1,1280,5120]{2,0,1:T(1,128)} async-done(((f32[1,1280,5120]{2,0,1:T(1,128)}), f32[1,1280,5120]{2,0,1:T(1,128)}) %all-reduce.16.cloned.1.call-update) | async-done | bytes 26214416
  2763.6 330.7 %reduce-scatter.6.cloned.1.call-done = f32[1,80,1280]{2,1,0:T(8,128)} async-done(((f32[1,5120,1280]{2,1,0:T(8,128)}), f32[1,80,1280]{2,1,0:T(8,128)}) %reduce-scatter.6.cloned.1.call-update) | async-done | bytes 409616 | tf_op jit(solution)/shard_map/reduce_scatter | solution.py:293
  (348 shorter events, 234.0 us)
Async XLA Ops:
  7.2 53.9 %all-gather.7.cloned.1.call-start = ((), (), s32[]{:S(2)}) async-start(), calls=%async_computation.2 | async-start | bytes 4915200 | tf_op jit(solution)/shard_map/all_gather | solution.py:213
  7.9 180.7 %all-gather.5.cloned.1.call-start = ((), (), s32[]{:S(2)}) async-start(), calls=%async_computation.1 | async-start | bytes 14745600 | tf_op jit(solution)/shard_map/all_gather | solution.py:212
  8.7 343.4 %all-gather.9.cloned.1.call-start = ((), (), s32[]{:S(2)}) async-start(), calls=%async_computation.3 | async-start | bytes 19660800 | tf_op jit(solution)/shard_map/all_gather | solution.py:214
  9.4 506.0 %copy-start.49 = (f32[1,1280]{1,0:T(1,128)S(1)}, f32[1,1280]{1,0:T(1,128)}, u32[]{:S(2)}) copy-start(f32[1,1280]{1,0:T(1,128)} %param.30) | copy-start | bytes 15364
  9.4 506.0 %copy-start.50 = (f32[1,1280]{1,0:T(1,128)S(1)}, f32[1,1280]{1,0:T(1,128)}, u32[]{:S(2)}) copy-start(f32[1,1280]{1,0:T(1,128)} %param.31) | copy-start | bytes 15364
  9.4 506.0 %copy-start.51 = (f32[1,1280]{1,0:T(1,128)S(1)}, f32[1,1280]{1,0:T(1,128)}, u32[]{:S(2)}) copy-start(f32[1,1280]{1,0:T(1,128)} %param.32) | copy-start | bytes 15364
  9.4 506.0 %copy-start.52 = (f32[1,1280]{1,0:T(1,128)S(1)}, f32[1,1280]{1,0:T(1,128)}, u32[]{:S(2)}) copy-start(f32[1,1280]{1,0:T(1,128)} %param.33) | copy-start | bytes 15364
  9.4 506.0 %copy-start.69 = (s32[2,1]{0,1:T(1,128)S(1)}, s32[2,1]{0,1:T(1,128)}, u32[]{:S(2)}) copy-start(s32[2,1]{0,1:T(1,128)} %param.24) | copy-start | bytes 28
  9.5 505.9 %all-gather.11.cloned.1.call-start = ((), (), s32[]{:S(2)}) async-start(), calls=%async_computation.4 | async-start | bytes 19660800 | tf_op jit(solution)/shard_map/all_gather | solution.py:215
  10.0 1517.4 %all-reduce.14.cloned.1.call-start = ((), (), s32[]{:S(2)}) async-start(), calls=%async_computation.7 | async-start | bytes 13107200
  515.7 13.8 copy-start.16
  552.9 17.6 collective-permute-start
  570.7 14.9 copy-start.14
  611.4 19.0 collective-permute-start.1
  681.1 84.9 %copy-start.53 = (f32[1280]{0:T(1024)}, f32[1280]{0:T(1024)S(1)}, u32[]{:S(2)}) copy-start(f32[1280]{0:T(1024)S(1)} %get-tuple-element.837) | copy-start | bytes 15364
  681.1 84.9 %copy-start.55 = (f32[1280]{0:T(1024)}, f32[1280]{0:T(1024)S(1)}, u32[]{:S(2)}) copy-start(f32[1280]{0:T(1024)S(1)} %get-tuple-element.840) | copy-start | bytes 15364
  681.1 84.9 %copy-start.57 = (f32[1280]{0:T(1024)}, f32[1280]{0:T(1024)S(1)}, u32[]{:S(2)}) copy-start(f32[1280]{0:T(1024)S(1)} %get-tuple-element.843) | copy-start | bytes 15364
  681.1 84.9 %copy-start.59 = (f32[1280]{0:T(1024)}, f32[1280]{0:T(1024)S(1)}, u32[]{:S(2)}) copy-start(f32[1280]{0:T(1024)S(1)} %get-tuple-element.846) | copy-start | bytes 15364
  681.1 83.0 %collective-permute-start.2 = (bf16[128,1280]{1,0:T(8,128)(2,1)}, bf16[128,1280]{1,0:T(8,128)(2,1)S(1)}, u32[]{:S(2)}, u32[]{:S(2)}) collective-permute-start(bf16[128,1280]{1,0:T(8,128)(2,1)} %get-tuple-element.822), channel_id=1, source_target_pairs={{64,0},{65,1},{66,2},{67,3},{68,4},{69,5},{70,6},{71,7},{72,8},{73... | collective-permute-start | bytes 983048 | tf_op jit(solution)/shard_map/ppermute | solution.py:15
  815.8 12.2 copy-start.24
  846.8 13.8 copy-start.61
  846.8 13.8 copy-start.63
  846.8 13.8 copy-start.65
  846.8 13.8 copy-start.67
  846.8 11.9 collective-permute-start.3
  874.2 10.1 copy-start.5
  910.7 12.2 copy-start.25
  962.4 1171.4 %all-reduce.12.cloned.1.call-start = ((), (), s32[]{:S(2)}) async-start(), calls=%async_computation.6 | async-start | bytes 39321600
  1011.8 1750.0 %all-reduce.16.cloned.1.call-start = ((), (), s32[]{:S(2)}) async-start(), calls=%async_computation.8 | async-start | bytes 52428800
  1068.2 2026.1 %reduce-scatter.6.cloned.1.call-start = ((), (), s32[]{:S(2)}) async-start(), calls=%async_computation.5 | async-start | bytes 26624000 | tf_op jit(solution)/shard_map/reduce_scatter | solution.py:293
  1107.1 1987.2 %copy-start.47 = (bf16[1,2,1,128,1280]{4,3,1,2,0:T(8,128)(2,1)}, bf16[1,2,1,128,1280]{4,3,1,2,0:T(8,128)(2,1)S(1)}, u32[]{:S(2)}) copy-start(bf16[1,2,1,128,1280]{4,3,1,2,0:T(8,128)(2,1)S(1)} %bitcast_dynamic-update-slice_fusion.9) | copy-start | bytes 1966084
  1389.3 1705.0 %copy-start.46 = (bf16[1,2,1,128,1280]{4,3,2,1,0:T(8,128)(2,1)}, bf16[1,2,1,128,1280]{4,3,2,1,0:T(8,128)(2,1)S(1)}, u32[]{:S(2)}) copy-start(bf16[1,2,1,128,1280]{4,3,2,1,0:T(8,128)(2,1)S(1)} %bitcast_dynamic-update-slice_fusion.10) | copy-start | bytes 1966084
  (38 other events, 153.5 us)
Sparse Core Ops, SparseCore 0:
  9.7 51.3 all-gather.6
  62.7 125.7 all-gather.4
  190.3 161.7 all-gather.8
  353.6 161.7 all-gather.10
  962.6 564.8 all-reduce.13
  1530.0 603.7 all-reduce.11
  2136.4 625.4 all-reduce.15
  2764.9 329.3 reduce-scatter.5
where the time goes:
time: 3110 us; the launch traced here: 3100 us
  waiting for transfers between devices  2300 us (74%)
  blocking collectives  277 us (9%)
  matrix products  208 us (7%)
  local copies, waits for them, and re-layouts  145 us (5%)
  other arithmetic  144 us (5%)
    unnamed x11, waiting for transfers between devices  1370 us
    reduce_scatter x1, waiting for transfers between devices, shards(): lax.psum_scatter(stacked[3], ('pair', 'dp'), scatter_dimension=1, tiled=T...  331 us
    unnamed x1, blocking collectives  277 us
    all_gather x1, waiting for transfers between devices, shards(): lax.all_gather(w_up, 'pair', axis=1, tiled=True)  163 us
    all_gather x1, waiting for transfers between devices, shards(): lax.all_gather(w_down, 'pair', axis=1, tiled=True)  163 us
    all_gather x1, waiting for transfers between devices, shards(): lax.all_gather(w_qkv, 'pair', axis=1, tiled=True)  128 us
    ppermute x4, waiting for transfers between devices, passed_along(): lax.ppermute(value, axis, [(source, source + steps) for source in range(i...  92.3 us
    add x7, other arithmetic, shards(): total_part + new_part  71.6 us
  transfers between devices with their start and end apart: 12, of which 10 were waited for; matrix products, arithmetic and copies ran while one was open for 6% of the time, Pallas kernels for 0%

commit v1 on v0

v1 whole, which is shorter than its diff:
```python
import functools

import jax
import jax.numpy as jnp
from jax import lax
from jax.experimental import pallas as pl
from jax.experimental.pallas import tpu as pltpu
from jax.sharding import PartitionSpec as P

D = 1280
FF = 5120
SEQ = 128
ROWS = 2 * SEQ
EPSILON = 1e-05
BF = jnp.bfloat16
F32 = jnp.float32
PIECE = 80

NN = (((1,), (0,)), ((), ()))
NT = (((1,), (1,)), ((), ()))
TN = (((0,), (0,)), ((), ()))


def dot(a, b, dims=NN):
    return lax.dot_general(a, b, dims, preferred_element_type=F32)


def row_blocks(count, body):
    def step(i, carry):
        body(pl.ds(pl.multiple_of(i * 32, 32), 32))
        return carry

    lax.fori_loop(0, count // 32, step, 0)


def stats(v):
    mean = jnp.mean(v, axis=-1, keepdims=True)
    centred = v - mean
    rstd = lax.rsqrt(jnp.mean(centred * centred, axis=-1, keepdims=True) + EPSILON)
    return centred * rstd, rstd


def start_square(pair, own, oth, which, dst, col, sem, group):
    pltpu.make_async_copy(
        own, dst.at[pl.ds(pl.multiple_of(pair * 640, 640), 640), pl.ds(col, D)], sem
    ).start()
    for r in range(8):
        row = pl.multiple_of((1 - pair) * 640 + r * PIECE, PIECE)
        pltpu.make_async_copy(
            oth.at[group * 8 + r, pl.ds(which * PIECE, PIECE)],
            dst.at[pl.ds(row, PIECE), pl.ds(col, D)],
            sem,
        ).start()


def start_tall(pair, own, oth, dst, sems):
    for u in range(2):
        pltpu.make_async_copy(
            own.at[pl.ds(u * D, D)],
            dst.at[pl.ds(pl.multiple_of(pair * 2560 + u * D, D), D)],
            sems.at[2 * pair + u],
        ).start()
    for d in range(32):
        row = pl.multiple_of((1 - pair) * 2560 + d * PIECE, PIECE)
        pltpu.make_async_copy(
            oth.at[d, pl.ds(2 * PIECE, PIECE)],
            dst.at[pl.ds(row, PIECE)],
            sems.at[2 * (1 - pair) + d // 16],
        ).start()


def wait_block(block, sem):
    pltpu.make_async_copy(block, block, sem).wait()


def start_attention_weights(pair, wqkv, wout, oth, w_ref, sems):
    for g in range(4):
        own = wqkv.at[:, pl.ds(g * D, D)] if g < 3 else wout
        start_square(pair, own, oth, 0, w_ref, g * D, sems.at[g], g)


def start_up(pair, wup, oth, w_ref, sems):
    for g in range(4):
        start_square(pair, wup.at[:, pl.ds(g * D, D)], oth, 1, w_ref, g * D, sems.at[g], g)


def attention_forward_kernel(
    ints, x_ref, g1, b1, g2, b2, wqkv, wout, oth,
    qkv_ref, prob_ref, mixed_ref, middle_ref, h1_ref, h2_ref,
    w_ref, sems,
):
    pair = ints[0]
    start_attention_weights(pair, wqkv, wout, oth, w_ref, sems)

    def norm_one(rows):
        hat, _ = stats(x_ref[rows, :].astype(F32))
        h1_ref[rows, :] = (hat * g1[...] + b1[...]).astype(BF)

    row_blocks(ROWS, norm_one)
    for g in range(3):
        wait_block(w_ref.at[:, pl.ds(g * D, D)], sems.at[g])

        def columns(n, carry):
            col = pl.ds(pl.multiple_of(g * D + n * 256, 256), 256)
            qkv_ref[:, col] = dot(h1_ref[...], w_ref[:, col]).astype(BF)
            return carry

        lax.fori_loop(0, 5, columns, 0)
    low = lax.broadcasted_iota(jnp.int32, (SEQ, 128), 1) < 64
    zero = jnp.zeros((SEQ, 128), BF)
    key_at = lax.broadcasted_iota(jnp.int32, (2 * SEQ, SEQ), 1)
    for s in range(2):
        valid = key_at < ints[1 + s]
        rows = pl.ds(s * SEQ, SEQ)

        def heads(i, carry):
            at = pl.multiple_of(i * 128, 128)
            q = qkv_ref[rows, pl.ds(at, 128)] * jnp.asarray(0.125, BF)
            k = qkv_ref[rows, pl.ds(at + D, 128)]
            v = qkv_ref[rows, pl.ds(at + 2 * D, 128)]
            both = jnp.concatenate([jnp.where(low, q, zero), jnp.where(low, zero, q)], axis=0)
            scores = jnp.where(valid, dot(both, k, NT), -1e30)
            raised = jnp.exp(scores - jnp.max(scores, axis=-1, keepdims=True))
            prob = (raised / jnp.sum(raised, axis=-1, keepdims=True)).astype(BF)
            prob_ref[s * 10 + i] = prob
            vv = jnp.concatenate([jnp.where(low, v, zero), jnp.where(low, zero, v)], axis=0)
            side = jnp.concatenate([prob[:SEQ], prob[SEQ:]], axis=1)
            mixed_ref[rows, pl.ds(at, 128)] = dot(side, vv).astype(BF)
            return carry

        lax.fori_loop(0, 10, heads, 0, unroll=2)
    wait_block(w_ref.at[:, pl.ds(3 * D, D)], sems.at[3])

    def out_columns(n, carry):
        col = pl.ds(pl.multiple_of(n * 256, 256), 256)
        wcol = pl.ds(pl.multiple_of(3 * D + n * 256, 256), 256)
        middle_ref[:, col] = x_ref[:, col].astype(F32) + dot(mixed_ref[...], w_ref[:, wcol])
        return carry

    lax.fori_loop(0, 5, out_columns, 0)

    def norm_two(rows):
        hat, _ = stats(middle_ref[rows, :])
        h2_ref[rows, :] = (hat * g2[...] + b2[...]).astype(BF)

    row_blocks(ROWS, norm_two)


def mlp_forward_kernel(
    ints, h2_ref, middle_ref, wup, wdown, oth, y_ref, active_ref, slope_ref, wu_ref, wd_ref, sems
):
    pair = ints[0]
    start_up(pair, wup, oth, wu_ref, sems)
    start_tall(pair, wdown, oth, wd_ref, sems.at[pl.ds(4, 4)])
    for g in range(4):
        wait_block(wu_ref.at[:, pl.ds(g * D, D)], sems.at[g])

        def columns(n, carry):
            col = pl.ds(pl.multiple_of(g * D + n * 256, 256), 256)
            u = dot(h2_ref[...], wu_ref[:, col])
            cdf = 0.5 + 0.5 * lax.erf(u * 0.7071067811865476)
            pdf = 0.3989422804014327 * jnp.exp(-0.5 * u * u)
            active_ref[:, col] = (u * cdf).astype(BF)
            slope_ref[:, col] = (cdf + u * pdf).astype(BF)
            return carry

        lax.fori_loop(0, 5, columns, 0)
    for g in range(4):
        wait_block(wd_ref.at[pl.ds(g * D, D)], sems.at[4 + g])

    def down_columns(n, carry):
        col = pl.ds(pl.multiple_of(n * 256, 256), 256)
        y_ref[:, col] = (middle_ref[:, col] + dot(active_ref[...], wd_ref[:, col])).astype(BF)
        return carry

    lax.fori_loop(0, 5, down_columns, 0)


def fold(total, value):
    for r in range(0, 32, 8):
        total = total + value[r : r + 8]
    return total


def norm_backward(grad_ref, value_of, gain, write, sums_ref):
    nothing = jnp.zeros((8, D), F32)

    def step(i, carry):
        of_gain, of_bias = carry
        rows = pl.ds(pl.multiple_of(i * 32, 32), 32)
        hat, rstd = stats(value_of(rows))
        grad = grad_ref[rows, :]
        scaled = grad * gain[...]
        first = jnp.mean(scaled, axis=-1, keepdims=True)
        second = jnp.mean(scaled * hat, axis=-1, keepdims=True)
        write(rows, rstd * (scaled - first - hat * second))
        return fold(of_gain, grad * hat), fold(of_bias, grad)

    of_gain, of_bias = lax.fori_loop(0, ROWS // 32, step, (nothing, nothing))
    sums_ref[0:1, :] = jnp.sum(of_gain, axis=0, keepdims=True)
    sums_ref[1:2, :] = jnp.sum(of_bias, axis=0, keepdims=True)


def mlp_backward_kernel(
    ints, grad_ref, slope_ref, middle_ref, g2, wup, wdown, oth,
    du_ref, dmiddle_ref, low_ref, sums_ref,
    wu_ref, wd_ref, dh_ref, sems,
):
    pair = ints[0]
    start_tall(pair, wdown, oth, wd_ref, sems.at[pl.ds(4, 4)])
    start_up(pair, wup, oth, wu_ref, sems)
    for g in range(4):
        wait_block(wd_ref.at[pl.ds(g * D, D)], sems.at[4 + g])

        def columns(n, carry):
            col = pl.ds(pl.multiple_of(g * D + n * 256, 256), 256)
            dact = dot(grad_ref[...], wd_ref[col, :], NT)
            du_ref[:, col] = (dact * slope_ref[:, col].astype(F32)).astype(BF)
            return carry

        lax.fori_loop(0, 5, columns, 0)
    for g in range(4):
        wait_block(wu_ref.at[:, pl.ds(g * D, D)], sems.at[g])

    def features(n, carry):
        at = pl.ds(pl.multiple_of(n * 256, 256), 256)
        dh_ref[:, at] = dot(du_ref[...], wu_ref[at, :], NT)
        return carry

    lax.fori_loop(0, 5, features, 0)

    def write(rows, grad):
        total = grad_ref[rows, :].astype(F32) + grad
        dmiddle_ref[rows, :] = total
        low_ref[rows, :] = total.astype(BF)

    norm_backward(dh_ref, lambda rows: middle_ref[rows, :], g2, write, sums_ref)


def attention_backward_kernel(
    ints, low_ref, dmiddle_ref, qkv_ref, prob_ref, x_ref, g1, wqkv, wout, oth,
    dqkv_ref, dx_ref, sums_ref,
    w_ref, dmixed_ref, dh_ref, sems,
):
    pair = ints[0]
    for g in (3, 0, 1, 2):
        own = wqkv.at[:, pl.ds(g * D, D)] if g < 3 else wout
        start_square(pair, own, oth, 0, w_ref, g * D, sems.at[g], g)
    wait_block(w_ref.at[:, pl.ds(3 * D, D)], sems.at[3])

    def out_features(n, carry):
        at = pl.ds(pl.multiple_of(n * 256, 256), 256)
        dmixed_ref[:, at] = dot(low_ref[...], w_ref[at, pl.ds(3 * D, D)], NT).astype(BF)
        return carry

    lax.fori_loop(0, 5, out_features, 0)
    low = lax.broadcasted_iota(jnp.int32, (SEQ, 128), 1) < 64
    zero = jnp.zeros((SEQ, 128), BF)

    def split(v):
        return jnp.concatenate([jnp.where(low, v, zero), jnp.where(low, zero, v)], axis=0)

    for s in range(2):
        rows = pl.ds(s * SEQ, SEQ)

        def heads(i, carry):
            at = pl.multiple_of(i * 128, 128)
            q = qkv_ref[rows, pl.ds(at, 128)] * jnp.asarray(0.125, BF)
            k = qkv_ref[rows, pl.ds(at + D, 128)] * jnp.asarray(0.125, BF)
            v = qkv_ref[rows, pl.ds(at + 2 * D, 128)]
            dm = split(dmixed_ref[rows, pl.ds(at, 128)])
            prob = prob_ref[s * 10 + i]
            dprob = dot(dm, v, NT)
            wide = prob.astype(F32)
            inner = jnp.sum(dprob * wide, axis=-1, keepdims=True)
            dscore = (wide * (dprob - inner)).astype(BF)
            side = jnp.concatenate([dscore[:SEQ], dscore[SEQ:]], axis=1)
            dqkv_ref[rows, pl.ds(at, 128)] = dot(side, split(k)).astype(BF)
            dqkv_ref[rows, pl.ds(at + D, 128)] = dot(dscore, split(q), TN).astype(BF)
            dqkv_ref[rows, pl.ds(at + 2 * D, 128)] = dot(prob, dm, TN).astype(BF)
            return carry

        lax.fori_loop(0, 10, heads, 0, unroll=2)
    for g in range(3):
        wait_block(w_ref.at[:, pl.ds(g * D, D)], sems.at[g])

    def features(n, carry):
        at = pl.ds(pl.multiple_of(n * 256, 256), 256)
        dh_ref[:, at] = dot(dqkv_ref[...], w_ref[at, pl.ds(0, 3 * D)], NT)
        return carry

    lax.fori_loop(0, 5, features, 0)

    def write(rows, grad):
        dx_ref[rows, :] = (dmiddle_ref[rows, :] + grad).astype(BF)

    norm_backward(dh_ref, lambda rows: x_ref[rows, :].astype(F32), g1, write, sums_ref)


def weight_grad_kernel(a_own, a_got, b_own, b_got, first, second):
    half = first.shape[0]
    for at, out in ((0, first), (half, second)):
        rows = pl.ds(at, half)
        out[...] = (
            dot(a_own[rows, :], b_own[...]) + dot(a_got[rows, :], b_got[...])
        ).astype(BF)


VM = pl.BlockSpec(memory_space=pltpu.VMEM)
SM = pl.BlockSpec(memory_space=pltpu.SMEM)
HB = pl.BlockSpec(memory_space=pl.ANY)
LIMIT = 60 * 1024 * 1024


def call(kernel, ins, outs, scratch, specs, flops, moved):
    return pl.pallas_call(
        kernel,
        out_shape=tuple(jax.ShapeDtypeStruct(s, t) for s, t in outs),
        in_specs=specs,
        out_specs=tuple(VM for _ in outs),
        scratch_shapes=scratch,
        compiler_params=pltpu.CompilerParams(vmem_limit_bytes=LIMIT),
        cost_estimate=pl.CostEstimate(flops=flops, bytes_accessed=moved, transcendentals=0),
    )(*ins)


def attention_forward(ints, x, norms, weights):
    g1, b1, g2, b2 = norms
    wqkv, wout, _, _, oth = weights
    return call(
        attention_forward_kernel,
        (ints, x, g1, b1, g2, b2, wqkv, wout, oth),
        [
            ((ROWS, 3 * D), BF), ((20, 2 * SEQ, SEQ), BF), ((ROWS, D), BF),
            ((ROWS, D), F32), ((ROWS, D), BF), ((ROWS, D), BF),
        ],
        [pltpu.VMEM((D, 4 * D), BF), pltpu.SemaphoreType.DMA((4,))],
        [SM, VM, VM, VM, VM, VM, HB, HB, HB],
        2 * ROWS * D * 4 * D, 14 * 2**20,
    )


def mlp_forward(ints, h2, middle, weights):
    _, _, wup, wdown, oth = weights
    return call(
        mlp_forward_kernel,
        (ints, h2, middle, wup, wdown, oth),
        [((ROWS, D), BF), ((ROWS, FF), BF), ((ROWS, FF), BF)],
        [pltpu.VMEM((D, FF), BF), pltpu.VMEM((FF, D), BF), pltpu.SemaphoreType.DMA((8,))],
        [SM, VM, VM, HB, HB, HB],
        4 * ROWS * D * FF, 32 * 2**20,
    )


def mlp_backward(ints, grad, slope, middle, g2, weights):
    _, _, wup, wdown, oth = weights
    return call(
        mlp_backward_kernel,
        (ints, grad, slope, middle, g2, wup, wdown, oth),
        [((ROWS, FF), BF), ((ROWS, D), F32), ((ROWS, D), BF), ((2, D), F32)],
        [
            pltpu.VMEM((D, FF), BF), pltpu.VMEM((FF, D), BF),
            pltpu.VMEM((ROWS, D), F32), pltpu.SemaphoreType.DMA((8,)),
        ],
        [SM, VM, VM, VM, VM, HB, HB, HB],
        4 * ROWS * D * FF, 32 * 2**20,
    )


def attention_backward(ints, low, dmiddle, qkv, prob, x, g1, weights):
    wqkv, wout, _, _, oth = weights
    return call(
        attention_backward_kernel,
        (ints, low, dmiddle, qkv, prob, x, g1, wqkv, wout, oth),
        [((ROWS, 3 * D), BF), ((ROWS, D), BF), ((2, D), F32)],
        [
            pltpu.VMEM((D, 4 * D), BF), pltpu.VMEM((ROWS, D), BF),
            pltpu.VMEM((ROWS, D), F32), pltpu.SemaphoreType.DMA((4,)),
        ],
        [SM, VM, VM, VM, VM, VM, VM, HB, HB, HB],
        2 * ROWS * D * 4 * D, 18 * 2**20,
    )


def weight_grad(a_own, a_got, b_own, b_got, tile):
    rows, k = a_own.shape
    cols = b_own.shape[1]
    whole = pl.BlockSpec((rows, k), lambda j: (0, 0))
    part = pl.BlockSpec((k, tile), lambda j: (0, j))
    out = pl.BlockSpec((rows // 2, tile), lambda j: (0, j))
    return pl.pallas_call(
        weight_grad_kernel,
        grid=(cols // tile,),
        out_shape=(jax.ShapeDtypeStruct((rows // 2, cols), BF),) * 2,
        in_specs=[whole, whole, part, part],
        out_specs=(out, out),
        compiler_params=pltpu.CompilerParams(vmem_limit_bytes=LIMIT),
        cost_estimate=pl.CostEstimate(
            flops=4 * rows * k * cols, bytes_accessed=2 * rows * cols, transcendentals=0
        ),
    )(a_own, a_got, b_own, b_got)


def dp_pairs(move):
    pairs = []
    for z in range(4):
        for y in range(4):
            for c in range(2):
                to = move(z, y, c)
                pairs.append((z * 8 + y * 2 + c, to[0] * 8 + to[1] * 2 + to[2]))
    return pairs


FLIPS = {
    ("y", 1): dp_pairs(lambda z, y, c: (z, y ^ 1, c)),
    ("y", 3): dp_pairs(lambda z, y, c: (z, y ^ 3, c)),
    ("z", 1): dp_pairs(lambda z, y, c: (z ^ 1, y, c)),
    ("z", 3): dp_pairs(lambda z, y, c: (z ^ 3, y, c)),
}
CORE = dp_pairs(lambda z, y, c: (z, y, 1 - c))
SWAP = [(0, 1), (1, 0)]
ORDERS = ((0, 3, 1, 2), (0, 1, 2, 3))


def add_low(a, b):
    return (a.astype(F32) + b.astype(F32)).astype(BF)


def reduce_axis(value, axis, parity, at):
    if parity == 0:
        flips = (1, 3)
        picks = (jnp.where((at == 0) | (at == 3), 0, 1), at // 2)
    else:
        flips = (3, 1)
        picks = (at // 2, at % 2)
    for flip, mine in zip(flips, picks):
        half = value.shape[0] // 2
        send = lax.dynamic_slice_in_dim(value, (1 - mine) * half, half, 0)
        got = lax.ppermute(send, "dp", FLIPS[axis, flip])
        value = add_low(lax.dynamic_slice_in_dim(value, mine * half, half, 0), got)
    return value


def reduce_plane(value, first, parity, at):
    second = "z" if first == "y" else "y"
    value = reduce_axis(value, first, parity, at[first])
    return reduce_axis(value, second, parity, at[second])


def reduce_both(halves, parity, at, pair):
    for_zero = reduce_plane(halves[0], "y", parity, at)
    for_one = reduce_plane(halves[1], "z", parity, at)
    send = jnp.where(pair == 0, for_one, for_zero)
    keep = jnp.where(pair == 0, for_zero, for_one)
    got = lax.ppermute(send, "pair", SWAP)
    return keep.astype(F32) + got.astype(F32)


def reduce_small(value):
    for axis, flip in (("y", 1), ("y", 3), ("z", 1), ("z", 3)):
        value = value + lax.ppermute(value, "dp", FLIPS[axis, flip])
    value = value + lax.ppermute(value, "dp", CORE)
    return value + lax.ppermute(value, "pair", SWAP)


def by_core(a, core):
    count = a.shape[1] // 64
    t = a.T.reshape(2, 4, 4, 2, count, ROWS)
    mine = lax.dynamic_index_in_dim(t, core, 3, keepdims=False)
    send = lax.dynamic_index_in_dim(t, 1 - core, 3, keepdims=False)
    return mine, send


def ordered(t, parity):
    order = ORDERS[parity]
    if parity == 0:
        t = jnp.stack([t[:, i] for i in order], axis=1)
        t = jnp.stack([t[:, :, i] for i in order], axis=2)
    first = jnp.swapaxes(t[0], 0, 1).reshape(-1, ROWS)
    return jnp.concatenate([first, t[1].reshape(-1, ROWS)], axis=0)


def shards(
    tokens, lengths, cotangent, w_qkv, w_out, w_up, w_down,
    norm1_gain, norm1_bias, norm2_gain, norm2_bias,
):
    section = lax.axis_index("section")
    pair = lax.axis_index("pair")
    place = lax.axis_index("dp")
    at = {"z": place // 8, "y": (place // 2) % 4}
    core = place % 2
    ints = jnp.concatenate([pair[None].astype(jnp.int32), lengths[:, 0]])
    norms = (norm1_gain, norm1_bias, norm2_gain, norm2_bias)
    x0 = tokens.reshape(ROWS, D)
    cot = cotangent.reshape(ROWS, D)
    wqkv, wout, wup, wdown = w_qkv[0], w_out[0], w_up[0], w_down[0]

    row = (place % 8) * PIECE
    att_piece = jnp.where(
        at["z"] == 3,
        lax.dynamic_slice(wout, (row, 0), (PIECE, D)),
        lax.dynamic_slice(wqkv, (row, jnp.minimum(at["z"], 2) * D), (PIECE, D)),
    )
    piece = jnp.concatenate(
        [
            att_piece,
            lax.dynamic_slice(wup, (row, at["z"] * D), (PIECE, D)),
            lax.dynamic_slice(wdown, (place * PIECE, 0), (PIECE, D)),
        ],
        axis=0,
    )
    oth = lax.all_gather(lax.ppermute(piece, "pair", SWAP), "dp", axis=0)
    weights = (wqkv, wout, wup, wdown, oth)

    def forward(x):
        qkv, prob, mixed, middle, h1, h2 = attention_forward(ints, x, norms, weights)
        y, active, slope = mlp_forward(ints, h2, middle, weights)
        return y, (x, qkv, prob, mixed, middle, h1, h2, active, slope)

    y, _ = forward(x0)
    arriving = lax.ppermute(y, "section", [(0, 1)])
    y, kept = forward(jnp.where(section == 0, x0, arriving))
    x, qkv, prob, mixed, middle, h1, h2, active, slope = kept

    def backward(grad):
        du, dmiddle, low, sums_two = mlp_backward(ints, grad, slope, middle, norms[2], weights)
        dqkv, dx, sums_one = attention_backward(
            ints, low, dmiddle, qkv, prob, x, norms[0], weights
        )
        return du, low, dqkv, dx, sums_one, sums_two

    arriving = lax.ppermute(backward(cot)[3], "section", [(1, 0)])

    features = [by_core(a, core) for a in (h1, mixed, h2, active)]
    lines = [m.size // ROWS for m, _ in features]
    got = lax.ppermute(
        jnp.concatenate([s.reshape(-1, ROWS) for _, s in features], axis=0), "dp", CORE
    )
    shared = []
    start = 0
    for (mine, _), count in zip(features, lines):
        shared.append((mine, got[start : start + count].reshape(mine.shape)))
        start += count
    rows_of = lambda which, parity: [ordered(t, parity) for t in shared[which]]
    h1_first, h1_second = rows_of(0, 0), rows_of(0, 1)
    mixed_rows, h2_rows, active_rows = rows_of(1, 1), rows_of(2, 0), rows_of(3, 1)

    grad = jnp.where(section == 0, arriving, cot)
    du, low, dqkv, dx, sums_one, sums_two = backward(grad)
    swap = lambda v: lax.ppermute(v, "dp", CORE)
    d_down = weight_grad(*active_rows, grad, swap(grad), 640)
    d_up = weight_grad(*h2_rows, du, swap(du), 1280)
    dqkv_got, low_got = swap(dqkv), swap(low)
    d_qk = weight_grad(*h1_first, dqkv[:, : 2 * D], dqkv_got[:, : 2 * D], 1280)
    d_v = weight_grad(*h1_second, dqkv[:, 2 * D :], dqkv_got[:, 2 * D :], 1280)
    d_out = weight_grad(*mixed_rows, low, low_got, 1280)
    d_vo = [jnp.concatenate([a, b], axis=1) for a, b in zip(d_v, d_out)]

    g_up = reduce_both(d_up, 0, at, pair)
    g_down = reduce_both(d_down, 1, at, pair)
    g_qk = reduce_both(d_qk, 0, at, pair)
    g_vo = reduce_both(d_vo, 1, at, pair)
    sums = reduce_small(jnp.concatenate([sums_one, sums_two], axis=0))
    sums = lax.dynamic_slice(sums, (0, (pair * 32 + place) * 20), (4, 20))
    return (
        y.reshape(1, 2, 1, SEQ, D),
        dx.reshape(1, 2, 1, SEQ, D),
        jnp.concatenate([g_qk, g_vo[:, :D]], axis=1)[None],
        g_vo[:, D:][None],
        g_up[None],
        g_down[None],
        sums[0:1],
        sums[1:2],
        sums[2:3],
        sums[3:4],
    )


def solution(mesh):
    rows = ("pair", "dp")
    in_specs = (
        P(None, rows, None, None),
        P(None, rows),
        P(None, rows, None, None),
        P("section", "pair", None),
        P("section", "pair", None),
        P("section", "pair", None),
        P("section", "pair", None),
        P("section", None),
        P("section", None),
        P("section", None),
        P("section", None),
    )
    out_specs = (
        P("section", None, rows, None, None),
        P("section", None, rows, None, None),
        P("section", rows, None),
        P("section", rows, None),
        P("section", rows, None),
        P("section", rows, None),
        P("section", rows),
        P("section", rows),
        P("section", rows),
        P("section", rows),
    )
    return jax.shard_map(shards, mesh=mesh, in_specs=in_specs, out_specs=out_specs, check_vma=False)
```

time: 3110 us -> 581 us (0.19)
  waiting for transfers between devices: 2300 us -> 223 us
  blocking collectives: 277 us -> 0 us
  matrix products: 208 us -> 0 us
  Pallas kernels: 0 us -> 191 us
  other arithmetic: 144 us -> 30.9 us
  local copies, waits for them, and re-layouts: 145 us -> 60.1 us
  starting transfers between devices: 5.85 us -> 53.3 us
    unnamed x11 -> x1, waiting for transfers between devices: 1370 us -> 0.02 us
    all_gather x4 -> x1, waiting for transfers between devices: 505 us -> 81.6 us  [shards(): oth = lax.all_gather(lax.ppermute(piece, 'pair', SWAP), 'dp', axis=0)]
    reduce_scatter x1 -> x0, waiting for transfers between devices: 331 us -> none  [shards(): lax.psum_scatter(stacked[3], ('pair', 'dp'), scatter_dimension=1, tiled=T...]
    unnamed x1 -> x0, blocking collectives: 277 us -> none
    dot_general x38 -> x0, matrix products: 208 us -> none  [the longest x2 30.1 us: layer_backward(): grad_down = jnp.dot(active.T, grad_low, preferred_element_type=jnp.float32)]
    pallas_call x0 -> x13, Pallas kernels: none -> 191 us  [the longest x8 165 us: call(): pl.pallas_call(kernel, out_shape=tuple((jax.ShapeDtypeStruct(s, t) for s,...]
    add x11 -> x8, other arithmetic: 72.2 us -> 0.36 us  [the longest x2 0.25 us: reduce_both(): return keep.astype(F32) + got.astype(F32)]
    broadcast_in_dim x11 -> x1, local copies, waits for them, and re-layouts: 56.8 us -> 0.02 us  [shards(): g_vo[:, D:][None]]
  transfers between devices with their start and end apart: 12 -> 51, of which waited for: 10 -> 29; matrix products, arithmetic and copies ran while one was open for 6% -> 13% of each run, Pallas kernels for 0% -> 12%
where the time goes in v1:
time: 581 us; the launch traced here: 574 us
  waiting for transfers between devices  223 us (38%)
  Pallas kernels  191 us (33%)
  local copies, waits for them, and re-layouts  60.1 us (10%)
  starting transfers between devices  53.3 us (9%)
  other arithmetic  30.9 us (5%)
  between operations  16 us (3%)
    pallas_call x8, Pallas kernels, call(): pl.pallas_call(kernel, out_shape=tuple((jax.ShapeDtypeStruct(s, t) for s,...  165 us
    ppermute x32, waiting for transfers between devices, reduce_axis(): got = lax.ppermute(send, 'dp', FLIPS[axis, flip])  91.4 us
    all_gather x1, waiting for transfers between devices, shards(): oth = lax.all_gather(lax.ppermute(piece, 'pair', SWAP), 'dp', axis=0)  81.6 us
    ppermute x32, starting transfers between devices, reduce_axis(): got = lax.ppermute(send, 'dp', FLIPS[axis, flip])  29.4 us
    pallas_call x5, Pallas kernels, weight_grad(): pl.pallas_call(weight_grad_kernel, grid=(cols // tile,), out_shape=(jax.S...  26.1 us
    ppermute x1, waiting for transfers between devices, shards(): oth = lax.all_gather(lax.ppermute(piece, 'pair', SWAP), 'dp', axis=0)  13.9 us
    ppermute x1, waiting for transfers between devices, shards(): arriving = lax.ppermute(y, 'section', [(0, 1)])  13.8 us
    ppermute x4, waiting for transfers between devices, reduce_both(): got = lax.ppermute(send, 'pair', SWAP)  13.8 us
  transfers between devices with their start and end apart: 51, of which 29 were waited for; matrix products, arithmetic and copies ran while one was open for 13% of the time, Pallas kernels for 12%

profile of v1, /device:TPU:0, one launch (start us, length us, event | category | flops | bytes accessed | tf_op | source)
XLA Modules:
  0.0 574.1 jit_solution(7380653322976386480)
XLA Ops:
  11.1 13.9 %collective-permute-done = bf16[240,1280]{1,0:T(8,128)(2,1)S(1)} collective-permute-done((bf16[240,1280]{1,0:T(8,128)(2,1)S(1)}, bf16[240,1280]{1,0:T(8,128)(2,1)S(1)}, u32[]{:S(2)}, u32[]{:S(2)}) %collective-permute-start) | collective-permute-done | bytes 614432 | tf_op jit(solution)/shard_map/ppermute | solution.py:512
  26.4 81.6 %all-gather.3.cloned.1.call-done = bf16[7680,1280]{1,0:T(8,128)(2,1)} async-done(((bf16[240,1280]{1,0:T(8,128)(2,1)}), bf16[7680,1280]{1,0:T(8,128)(2,1)}) %all-gather.3.cloned.1.call-update) | async-done | bytes 19660816 | tf_op jit(solution)/shard_map/all_gather | solution.py:512
  108.0 22.6 %shard_map.186 = (bf16[256,3840]{1,0:T(8,128)(2,1)}, bf16[20,256,128]{2,1,0:T(8,128)(2,1)}, bf16[256,1280]{1,0:T(8,128)(2,1)}, f32[256,1280]{1,0:T(8,128)}, bf16...) custom-call(s32[3]{0:T(128)} %pad_add_fusion.ints, bf16[256,1280]{1,0:T(8,128)(2,1)} %bitcast.104, f32[1,1280]{1,0:T(1,128)} %g1.7, ...), custom_call_target="tpu_custom_call" | custom-call | flops 3355443200 | bytes 14680064 | tf_op jit(solution)/shard_map/pallas_call | solution.py:316
  130.6 17.8 %shard_map.187 = (bf16[256,1280]{1,0:T(8,128)(2,1)}, bf16[256,5120]{1,0:T(8,128)(2,1)}, bf16[256,5120]{1,0:T(8,128)(2,1)}) custom-call(s32[3]{0:T(128)} %pad_add_fusion.ints, bf16[256,1280]{1,0:T(8,128)(2,1)} %get-tuple-element.42.h2_ref, f32[256,1280]{1,0:T(8,128)} %get-tuple-element.43.middle_ref, bf16[640,5120]{1,0:T(8,128)(2,1)} %bitcast.89, ...), custom_call_target="tpu_custom_call" | custom-call | flops 6710886400 | bytes 33554432 | tf_op jit(solution)/shard_map/pallas_call | solution.py:316
  148.5 5.4 collective-permute-start.1
  154.3 13.8 %collective-permute-done.1 = bf16[256,1280]{1,0:T(8,128)(2,1)S(1)} collective-permute-done((bf16[256,1280]{1,0:T(8,128)(2,1)}, bf16[256,1280]{1,0:T(8,128)(2,1)S(1)}, u32[]{:S(2)}, u32[]{:S(2)}) %collective-permute-start.1) | collective-permute-done | bytes 655392 | tf_op jit(solution)/shard_map/ppermute | solution.py:521
  169.0 22.6 %shard_map.188 = (bf16[256,3840]{1,0:T(8,128)(2,1)}, bf16[20,256,128]{2,1,0:T(8,128)(2,1)}, bf16[256,1280]{1,0:T(8,128)(2,1)}, f32[256,1280]{1,0:T(8,128)}, bf16...) custom-call(s32[3]{0:T(128)} %pad_add_fusion.ints, bf16[256,1280]{1,0:T(8,128)(2,1)} %broadcast_select_fusion.1.x_ref, ...), custom_call_target="tpu_custom_call" | custom-call | flops 3355443200 | bytes 14680064 | tf_op jit(solution)/shard_map/pallas_call | solution.py:316
  197.8 17.8 %shard_map.189 = (bf16[256,1280]{1,0:T(8,128)(2,1)}, bf16[256,5120]{1,0:T(8,128)(2,1)}, bf16[256,5120]{1,0:T(8,128)(2,1)}) custom-call(s32[3]{0:T(128)} %pad_add_fusion.ints, bf16[256,1280]{1,0:T(8,128)(2,1)} %get-tuple-element.45.h2_ref, f32[256,1280]{1,0:T(8,128)} %get-tuple-element.46.middle_ref, bf16[640,5120]{1,0:T(8,128)(2,1)} %bitcast.90, ...), custom_call_target="tpu_custom_call" | custom-call | flops 6710886400 | bytes 33554432 | tf_op jit(solution)/shard_map/pallas_call | solution.py:316
  215.6 20.5 %shard_map.190 = (bf16[256,5120]{1,0:T(8,128)(2,1)}, f32[256,1280]{1,0:T(8,128)}, bf16[256,1280]{1,0:T(8,128)(2,1)}, f32[2,1280]{1,0:T(2,128)}) custom-call(s32[3]{0:T(128)} %pad_add_fusion.ints, bf16[256,1280]{1,0:T(8,128)(2,1)} %bitcast.110, bf16[256,5120]{1,0:T(8,128)(2,1)} %get-tuple-element.48.slope_ref, f32[256,1280]{1,0:T(8,128)} %get-tuple-element.46.middle_ref, ...), custom_call_target="tpu_custom_call" | custom-call | flops 6710886400 | bytes 33554432 | tf_op jit(solution)/shard_map/pallas_call | solution.py:316
  236.1 21.4 %shard_map.191 = (bf16[256,3840]{1,0:T(8,128)(2,1)}, bf16[256,1280]{1,0:T(8,128)(2,1)}, f32[2,1280]{1,0:T(2,128)}) custom-call(s32[3]{0:T(128)} %pad_add_fusion.ints, bf16[256,1280]{1,0:T(8,128)(2,1)} %get-tuple-element.49.low_ref, f32[256,1280]{1,0:T(8,128)} %get-tuple-element.50.dmiddle_ref, bf16[256,3840]{1,0:T(8,128)(2,1)} %get-tuple-element.51.qkv_ref, ...), custom_call_target="tpu_custom_call" | custom-call | flops 3355443200 | bytes 18874368 | tf_op jit(solution)/shard_map/pallas_call | solution.py:316
  274.2 3.2 pad_maximum_fusion
  285.7 20.4 %shard_map.192 = (bf16[256,5120]{1,0:T(8,128)(2,1)}, f32[256,1280]{1,0:T(8,128)}, bf16[256,1280]{1,0:T(8,128)(2,1)}, f32[2,1280]{1,0:T(2,128)}) custom-call(s32[3]{0:T(128)} %pad_add_fusion.ints, bf16[256,1280]{1,0:T(8,128)(2,1)} %broadcast_select_fusion.grad_ref.b_own, bf16[256,5120]{1,0:T(8,128)(2,1)} %get-tuple-element.48.slope_ref, ...), custom_call_target="tpu_custom_call" | custom-call | flops 6710886400 | bytes 33554432 | tf_op jit(solution)/shard_map/pallas_call | solution.py:316
  306.2 21.4 %shard_map.193 = (bf16[256,3840]{1,0:T(8,128)(2,1)}, bf16[256,1280]{1,0:T(8,128)(2,1)}, f32[2,1280]{1,0:T(2,128)}) custom-call(s32[3]{0:T(128)} %pad_add_fusion.ints, bf16[256,1280]{1,0:T(8,128)(2,1)} %get-tuple-element.54.low_ref.b_own, f32[256,1280]{1,0:T(8,128)} %get-tuple-element.55.dmiddle_ref, bf16[256,3840]{1,0:T(8,128)(2,1)} %get-tuple-element.51.qkv_ref, ...), custom_call_target="tpu_custom_call" | custom-call | flops 3355443200 | bytes 18874368 | tf_op jit(solution)/shard_map/pallas_call | solution.py:316
  347.6 4.3 collective-permute-start.49
  362.6 7.7 %shard_map.198 = (bf16[1280,1280]{1,0:T(8,128)(2,1)}, bf16[1280,1280]{1,0:T(8,128)(2,1)}) custom-call(bf16[2560,256]{1,0:T(8,128)(2,1)} %pad_maximum_fusion.1.a_own, bf16[2560,256]{1,0:T(8,128)(2,1)} %pad_maximum_fusion.2.a_got, bf16[256,1280]{1,0:T(8,128)(2,1)} %broadcast_select_fusion.grad_ref.b_own, bf16[256,1280]{1,0:T(8,128)(2,1)} %collective-permute-done.34.b_got), custom_call_target="tpu_custom_call" | custom-call | flops 3355443200 | bytes 6553600 | tf_op jit(solution)/shard_map/pallas_call | solution.py:391
  380.8 3.4 shard_map.196
  388.9 4.5 shard_map.194
  397.8 3.4 shard_map.195
  408.3 7.2 %shard_map.197 = (bf16[320,5120]{1,0:T(8,128)(2,1)}, bf16[320,5120]{1,0:T(8,128)(2,1)}) custom-call(bf16[640,256]{1,0:T(8,128)(2,1)} %pad_maximum_fusion.10.a_own, bf16[640,256]{1,0:T(8,128)(2,1)} %pad_maximum_fusion.11.a_got, bf16[256,5120]{1,0:T(8,128)(2,1)} %get-tuple-element.67.b_own, bf16[256,5120]{1,0:T(8,128)(2,1)} %collective-permute-done.24.b_got), custom_call_target="tpu_custom_call" | custom-call | flops 3355443200 | bytes 6553600 | tf_op jit(solution)/shard_map/pallas_call | solution.py:391
  423.9 5.9 %collective-permute-done.19 = bf16[160,2560]{1,0:T(8,128)(2,1)} collective-permute-done((bf16[160,2560]{1,0:T(8,128)(2,1)}, bf16[160,2560]{1,0:T(8,128)(2,1)}, u32[]{:S(2)}, u32[]{:S(2)}) %collective-permute-start.19) | collective-permute-done | bytes 819232 | tf_op jit(solution)/shard_map/ppermute | solution.py:439
  431.5 8.1 %collective-permute-done.15 = bf16[160,2560]{1,0:T(8,128)(2,1)S(1)} collective-permute-done((bf16[160,2560]{1,0:T(8,128)(2,1)S(1)}, bf16[160,2560]{1,0:T(8,128)(2,1)S(1)}, u32[]{:S(2)}, u32[]{:S(2)}) %collective-permute-start.15) | collective-permute-done | bytes 819232 | tf_op jit(solution)/shard_map/ppermute | solution.py:439
  440.6 9.8 %collective-permute-done.10 = bf16[80,2560]{1,0:T(8,128)(2,1)S(1)} collective-permute-done((bf16[80,2560]{1,0:T(8,128)(2,1)S(1)}, bf16[80,2560]{1,0:T(8,128)(2,1)S(1)}, u32[]{:S(2)}, u32[]{:S(2)}) %collective-permute-start.10) | collective-permute-done | bytes 409632 | tf_op jit(solution)/shard_map/ppermute | solution.py:439
  451.0 9.3 %collective-permute-done.6 = bf16[80,2560]{1,0:T(8,128)(2,1)S(1)} collective-permute-done((bf16[80,2560]{1,0:T(8,128)(2,1)S(1)}, bf16[80,2560]{1,0:T(8,128)(2,1)S(1)}, u32[]{:S(2)}, u32[]{:S(2)}) %collective-permute-start.6) | collective-permute-done | bytes 409632 | tf_op jit(solution)/shard_map/ppermute | solution.py:439
  460.4 7.8 %collective-permute-done.20 = bf16[80,2560]{1,0:T(8,128)(2,1)S(1)} collective-permute-done((bf16[80,2560]{1,0:T(8,128)(2,1)S(1)}, bf16[80,2560]{1,0:T(8,128)(2,1)S(1)}, u32[]{:S(2)}, u32[]{:S(2)}) %collective-permute-start.20) | collective-permute-done | bytes 409632 | tf_op jit(solution)/shard_map/ppermute | solution.py:439
  468.6 9.8 %collective-permute-done.16 = bf16[80,2560]{1,0:T(8,128)(2,1)S(1)} collective-permute-done((bf16[80,2560]{1,0:T(8,128)(2,1)S(1)}, bf16[80,2560]{1,0:T(8,128)(2,1)S(1)}, u32[]{:S(2)}, u32[]{:S(2)}) %collective-permute-start.16) | collective-permute-done | bytes 409632 | tf_op jit(solution)/shard_map/ppermute | solution.py:439
  496.1 3.5 collective-permute-done.8
  505.2 4.5 collective-permute-done.13
  510.1 4.5 collective-permute-done.23
  525.0 5.5 collective-permute-done.41
  532.4 8.5 %collective-permute-done.30 = bf16[80,5120]{1,0:T(8,128)(2,1)S(1)} collective-permute-done((bf16[80,5120]{1,0:T(8,128)(2,1)S(1)}, bf16[80,5120]{1,0:T(8,128)(2,1)S(1)}, u32[]{:S(2)}, u32[]{:S(2)}) %collective-permute-start.30) | collective-permute-done | bytes 819232 | tf_op jit(solution)/shard_map/ppermute | solution.py:439
  542.5 6.7 %collective-permute-done.31 = bf16[40,5120]{1,0:T(8,128)(2,1)S(1)} collective-permute-done((bf16[40,5120]{1,0:T(8,128)(2,1)S(1)}, bf16[40,5120]{1,0:T(8,128)(2,1)S(1)}, u32[]{:S(2)}, u32[]{:S(2)}) %collective-permute-start.31) | collective-permute-done | bytes 409632 | tf_op jit(solution)/shard_map/ppermute | solution.py:439
  560.6 4.8 collective-permute-done.33
  (317 shorter events, 156.4 us)
Async XLA Ops:
  7.2 100.9 %all-gather.3.cloned.1.call-start = ((), (), s32[]{:S(2)}) async-start(), calls=%async_computation | async-start | bytes 20275200 | tf_op jit(solution)/shard_map/all_gather | solution.py:512
  9.5 15.5 %collective-permute-start = (bf16[240,1280]{1,0:T(8,128)(2,1)S(1)}, bf16[240,1280]{1,0:T(8,128)(2,1)S(1)}, u32[]{:S(2)}, u32[]{:S(2)}) collective-permute-start(bf16[240,1280]{1,0:T(8,128)(2,1)S(1)} %pad_maximum_fusion.3), channel_id=1, source_target_pairs={{0,32},{32,0},{1,33},{33,1},{2,34},{34,2},{3,35},{35,3},{4,36},{36... | collective-permute-start | bytes 1843208 | tf_op jit(solution)/shard_map/ppermute | solution.py:512
  148.5 19.6 %collective-permute-start.1 = (bf16[256,1280]{1,0:T(8,128)(2,1)}, bf16[256,1280]{1,0:T(8,128)(2,1)S(1)}, u32[]{:S(2)}, u32[]{:S(2)}) collective-permute-start(bf16[256,1280]{1,0:T(8,128)(2,1)} %get-tuple-element.44), channel_id=1, source_target_pairs={{0,64},{1,65},{2,66},{3,67},{4,68},{5,69},{6,70},{7,71},{8,72},{9,... | collective-permute-start | bytes 1966088 | tf_op jit(solution)/shard_map/ppermute | solution.py:521
  257.5 26.2 %collective-permute-start.2 = (bf16[256,1280]{1,0:T(8,128)(2,1)}, bf16[256,1280]{1,0:T(8,128)(2,1)}, u32[]{:S(2)}, u32[]{:S(2)}) collective-permute-start(bf16[256,1280]{1,0:T(8,128)(2,1)} %get-tuple-element.53), channel_id=1, source_target_pairs={{64,0},{65,1},{66,2},{67,3},{68,4},{69,5},{70,6},{71,7},{72,8},{73... | collective-permute-start | bytes 1966088 | tf_op jit(solution)/shard_map/ppermute | solution.py:532
  277.4 81.3 %collective-permute-start.3 = (bf16[4480,256]{1,0:T(8,128)(2,1)}, bf16[4480,256]{1,0:T(8,128)(2,1)}, u32[]{:S(2)}, u32[]{:S(2)}) collective-permute-start(bf16[4480,256]{1,0:T(8,128)(2,1)} %pad_maximum_fusion), channel_id=1, source_target_pairs={{0,1},{1,0},{2,3},{3,2},{4,5},{5,4},{6,7},{7,6},{8,9},{9,8},{10,11... | collective-permute-start | bytes 6881288 | tf_op jit(solution)/shard_map/ppermute | solution.py:536
  347.6 10.0 %collective-permute-start.49 = (f32[4,1280]{1,0:T(4,128)S(1)}, f32[4,1280]{1,0:T(4,128)S(1)}, u32[]{:S(2)}, u32[]{:S(2)}) collective-permute-start(f32[4,1280]{1,0:T(4,128)S(1)} %add.422), channel_id=1, source_target_pairs={{0,32},{32,0},{1,33},{33,1},{2,34},{34,2},{3,35},{35,3},{4,36},{36... | collective-permute-start | bytes 61448 | tf_op jit(solution)/shard_map/ppermute | solution.py:463
  352.7 9.9 %collective-permute-start.34 = (bf16[256,1280]{1,0:T(8,128)(2,1)S(1)}, bf16[256,1280]{1,0:T(8,128)(2,1)}, u32[]{:S(2)}, u32[]{:S(2)}) collective-permute-start(bf16[256,1280]{1,0:T(8,128)(2,1)S(1)} %copy-done.9), channel_id=1, source_target_pairs={{0,1},{1,0},{2,3},{3,2},{4,5},{5,4},{6,7},{7,6},{8,9},{9,8},{10,11... | collective-permute-start | bytes 1966088 | tf_op jit(solution)/shard_map/ppermute | solution.py:550
  352.7 33.8 %collective-permute-start.4 = (bf16[256,3840]{1,0:T(8,128)(2,1)}, bf16[256,3840]{1,0:T(8,128)(2,1)}, u32[]{:S(2)}, u32[]{:S(2)}) collective-permute-start(bf16[256,3840]{1,0:T(8,128)(2,1)} %get-tuple-element.60), channel_id=1, source_target_pairs={{0,1},{1,0},{2,3},{3,2},{4,5},{5,4},{6,7},{7,6},{8,9},{9,8},{10,11... | collective-permute-start | bytes 5898248 | tf_op jit(solution)/shard_map/ppermute | solution.py:550
  355.6 25.2 %collective-permute-start.14 = (bf16[256,1280]{1,0:T(8,128)(2,1)}, bf16[256,1280]{1,0:T(8,128)(2,1)}, u32[]{:S(2)}, u32[]{:S(2)}) collective-permute-start(bf16[256,1280]{1,0:T(8,128)(2,1)} %get-tuple-element.54.low_ref.b_own), channel_id=1, source_target_pairs={{0,1},{1,0},{2,3},{3,2},{4,5},{5,4},{6,7},{7,6},{8,9},{9,8},{10,11... | collective-permute-start | bytes 1966088 | tf_op jit(solution)/shard_map/ppermute | solution.py:550
  357.6 48.2 %collective-permute-start.24 = (bf16[256,5120]{1,0:T(8,128)(2,1)}, bf16[256,5120]{1,0:T(8,128)(2,1)}, u32[]{:S(2)}, u32[]{:S(2)}) collective-permute-start(bf16[256,5120]{1,0:T(8,128)(2,1)} %get-tuple-element.67.b_own), channel_id=1, source_target_pairs={{0,1},{1,0},{2,3},{3,2},{4,5},{5,4},{6,7},{7,6},{8,9},{9,8},{10,11... | collective-permute-start | bytes 7864328 | tf_op jit(solution)/shard_map/ppermute | solution.py:550
  373.1 105.5 %collective-permute-start.39 = (bf16[640,1280]{1,0:T(8,128)(2,1)}, bf16[640,1280]{1,0:T(8,128)(2,1)}, u32[]{:S(2)}, u32[]{:S(2)}) collective-permute-start(bf16[640,1280]{1,0:T(8,128)(2,1)} %constant_dynamic-slice_fusion.6), channel_id=1, source_target_pairs={{0,24},{1,25},{2,26},{3,27},{4,28},{5,29},{6,30},{7,31},{8,16},{9,... | collective-permute-start | bytes 4915208 | tf_op jit(solution)/shard_map/ppermute | solution.py:439
  376.8 104.9 %collective-permute-start.35 = (bf16[640,1280]{1,0:T(8,128)(2,1)}, bf16[640,1280]{1,0:T(8,128)(2,1)}, u32[]{:S(2)}, u32[]{:S(2)}) collective-permute-start(bf16[640,1280]{1,0:T(8,128)(2,1)} %constant_dynamic-slice_fusion.10), channel_id=1, source_target_pairs={{0,6},{1,7},{2,4},{3,5},{4,2},{5,3},{6,0},{7,1},{8,14},{9,15},{10,... | collective-permute-start | bytes 4915208 | tf_op jit(solution)/shard_map/ppermute | solution.py:439
  395.6 22.4 %collective-permute-start.9 = (bf16[160,2560]{1,0:T(8,128)(2,1)}, bf16[160,2560]{1,0:T(8,128)(2,1)}, u32[]{:S(2)}, u32[]{:S(2)}) collective-permute-start(bf16[160,2560]{1,0:T(8,128)(2,1)} %constant_dynamic-slice_fusion.32), channel_id=1, source_target_pairs={{0,8},{1,9},{2,10},{3,11},{4,12},{5,13},{6,14},{7,15},{8,0},{9,1},... | collective-permute-start | bytes 2457608 | tf_op jit(solution)/shard_map/ppermute | solution.py:439
  395.7 25.3 %collective-permute-start.5 = (bf16[160,2560]{1,0:T(8,128)(2,1)S(1)}, bf16[160,2560]{1,0:T(8,128)(2,1)}, u32[]{:S(2)}, u32[]{:S(2)}) collective-permute-start(bf16[160,2560]{1,0:T(8,128)(2,1)S(1)} %constant_dynamic-slice_fusion.36), channel_id=1, source_target_pairs={{0,2},{1,3},{2,0},{3,1},{4,6},{5,7},{6,4},{7,5},{8,10},{9,11},{10,... | collective-permute-start | bytes 2457608 | tf_op jit(solution)/shard_map/ppermute | solution.py:439
  405.8 24.1 %collective-permute-start.19 = (bf16[160,2560]{1,0:T(8,128)(2,1)}, bf16[160,2560]{1,0:T(8,128)(2,1)}, u32[]{:S(2)}, u32[]{:S(2)}) collective-permute-start(bf16[160,2560]{1,0:T(8,128)(2,1)} %constant_dynamic-slice_fusion.23), channel_id=1, source_target_pairs={{0,24},{1,25},{2,26},{3,27},{4,28},{5,29},{6,30},{7,31},{8,16},{9,... | collective-permute-start | bytes 2457608 | tf_op jit(solution)/shard_map/ppermute | solution.py:439
  419.1 20.5 %collective-permute-start.15 = (bf16[160,2560]{1,0:T(8,128)(2,1)S(1)}, bf16[160,2560]{1,0:T(8,128)(2,1)S(1)}, u32[]{:S(2)}, u32[]{:S(2)}) collective-permute-start(bf16[160,2560]{1,0:T(8,128)(2,1)S(1)} %copy-done.17), channel_id=1, source_target_pairs={{0,6},{1,7},{2,4},{3,5},{4,2},{5,3},{6,0},{7,1},{8,14},{9,15},{10,... | collective-permute-start | bytes 2457608 | tf_op jit(solution)/shard_map/ppermute | solution.py:439
  421.0 100.0 %collective-permute-start.29 = (bf16[160,5120]{1,0:T(8,128)(2,1)S(1)}, bf16[160,5120]{1,0:T(8,128)(2,1)S(1)}, u32[]{:S(2)}, u32[]{:S(2)}) collective-permute-start(bf16[160,5120]{1,0:T(8,128)(2,1)S(1)} %constant_dynamic-slice_fusion.15), channel_id=1, source_target_pairs={{0,8},{1,9},{2,10},{3,11},{4,12},{5,13},{6,14},{7,15},{8,0},{9,1},... | collective-permute-start | bytes 4915208 | tf_op jit(solution)/shard_map/ppermute | solution.py:439
  429.9 92.7 %collective-permute-start.25 = (bf16[160,5120]{1,0:T(8,128)(2,1)S(1)}, bf16[160,5120]{1,0:T(8,128)(2,1)S(1)}, u32[]{:S(2)}, u32[]{:S(2)}) collective-permute-start(bf16[160,5120]{1,0:T(8,128)(2,1)S(1)} %constant_dynamic-slice_fusion.19), channel_id=1, source_target_pairs={{0,2},{1,3},{2,0},{3,1},{4,6},{5,7},{6,4},{7,5},{8,10},{9,11},{10,... | collective-permute-start | bytes 4915208 | tf_op jit(solution)/shard_map/ppermute | solution.py:439
  439.6 10.8 %collective-permute-start.10 = (bf16[80,2560]{1,0:T(8,128)(2,1)S(1)}, bf16[80,2560]{1,0:T(8,128)(2,1)S(1)}, u32[]{:S(2)}, u32[]{:S(2)}) collective-permute-start(bf16[80,2560]{1,0:T(8,128)(2,1)S(1)} %constant_dynamic-slice_fusion.31), channel_id=1, source_target_pairs={{0,24},{1,25},{2,26},{3,27},{4,28},{5,29},{6,30},{7,31},{8,16},{9,... | collective-permute-start | bytes 1228808 | tf_op jit(solution)/shard_map/ppermute | solution.py:439
  450.4 9.9 %collective-permute-start.6 = (bf16[80,2560]{1,0:T(8,128)(2,1)S(1)}, bf16[80,2560]{1,0:T(8,128)(2,1)S(1)}, u32[]{:S(2)}, u32[]{:S(2)}) collective-permute-start(bf16[80,2560]{1,0:T(8,128)(2,1)S(1)} %constant_dynamic-slice_fusion.35), channel_id=1, source_target_pairs={{0,6},{1,7},{2,4},{3,5},{4,2},{5,3},{6,0},{7,1},{8,14},{9,15},{10,... | collective-permute-start | bytes 1228808 | tf_op jit(solution)/shard_map/ppermute | solution.py:439
  468.3 10.1 %collective-permute-start.16 = (bf16[80,2560]{1,0:T(8,128)(2,1)S(1)}, bf16[80,2560]{1,0:T(8,128)(2,1)S(1)}, u32[]{:S(2)}, u32[]{:S(2)}) collective-permute-start(bf16[80,2560]{1,0:T(8,128)(2,1)S(1)} %constant_dynamic-slice_fusion.26), channel_id=1, source_target_pairs={{0,2},{1,3},{2,0},{3,1},{4,6},{5,7},{6,4},{7,5},{8,10},{9,11},{10,... | collective-permute-start | bytes 1228808 | tf_op jit(solution)/shard_map/ppermute | solution.py:439
  478.6 8.1 %collective-permute-start.7 = (bf16[40,2560]{1,0:T(8,128)(2,1)S(1)}, bf16[40,2560]{1,0:T(8,128)(2,1)S(1)}, u32[]{:S(2)}, u32[]{:S(2)}) collective-permute-start(bf16[40,2560]{1,0:T(8,128)(2,1)S(1)} %constant_dynamic-slice_fusion.34), channel_id=1, source_target_pairs={{0,8},{1,9},{2,10},{3,11},{4,12},{5,13},{6,14},{7,15},{8,0},{9,1},... | collective-permute-start | bytes 614408 | tf_op jit(solution)/shard_map/ppermute | solution.py:439
  481.7 8.4 %collective-permute-start.21 = (bf16[40,2560]{1,0:T(8,128)(2,1)S(1)}, bf16[40,2560]{1,0:T(8,128)(2,1)S(1)}, u32[]{:S(2)}, u32[]{:S(2)}) collective-permute-start(bf16[40,2560]{1,0:T(8,128)(2,1)S(1)} %constant_dynamic-slice_fusion.21), channel_id=1, source_target_pairs={{0,6},{1,7},{2,4},{3,5},{4,2},{5,3},{6,0},{7,1},{8,14},{9,15},{10,... | collective-permute-start | bytes 614408 | tf_op jit(solution)/shard_map/ppermute | solution.py:439
  486.7 29.8 %collective-permute-start.40 = (bf16[320,1280]{1,0:T(8,128)(2,1)S(1)}, bf16[320,1280]{1,0:T(8,128)(2,1)S(1)}, u32[]{:S(2)}, u32[]{:S(2)}) collective-permute-start(bf16[320,1280]{1,0:T(8,128)(2,1)S(1)} %constant_dynamic-slice_fusion.5), channel_id=1, source_target_pairs={{0,8},{1,9},{2,10},{3,11},{4,12},{5,13},{6,14},{7,15},{8,0},{9,1},... | collective-permute-start | bytes 2457608 | tf_op jit(solution)/shard_map/ppermute | solution.py:439
  502.4 16.0 %collective-permute-start.36 = (bf16[320,1280]{1,0:T(8,128)(2,1)S(1)}, bf16[320,1280]{1,0:T(8,128)(2,1)S(1)}, u32[]{:S(2)}, u32[]{:S(2)}) collective-permute-start(bf16[320,1280]{1,0:T(8,128)(2,1)S(1)} %constant_dynamic-slice_fusion.9), channel_id=1, source_target_pairs={{0,2},{1,3},{2,0},{3,1},{4,6},{5,7},{6,4},{7,5},{8,10},{9,11},{10,... | collective-permute-start | bytes 2457608 | tf_op jit(solution)/shard_map/ppermute | solution.py:439
  516.8 13.7 %collective-permute-start.41 = (bf16[160,1280]{1,0:T(8,128)(2,1)S(1)}, bf16[160,1280]{1,0:T(8,128)(2,1)S(1)}, u32[]{:S(2)}, u32[]{:S(2)}) collective-permute-start(bf16[160,1280]{1,0:T(8,128)(2,1)S(1)} %constant_dynamic-slice_fusion.4), channel_id=1, source_target_pairs={{0,6},{1,7},{2,4},{3,5},{4,2},{5,3},{6,0},{7,1},{8,14},{9,15},{10,... | collective-permute-start | bytes 1228808 | tf_op jit(solution)/shard_map/ppermute | solution.py:439
  518.6 13.5 %collective-permute-start.37 = (bf16[160,1280]{1,0:T(8,128)(2,1)S(1)}, bf16[160,1280]{1,0:T(8,128)(2,1)S(1)}, u32[]{:S(2)}, u32[]{:S(2)}) collective-permute-start(bf16[160,1280]{1,0:T(8,128)(2,1)S(1)} %constant_dynamic-slice_fusion.8), channel_id=1, source_target_pairs={{0,24},{1,25},{2,26},{3,27},{4,28},{5,29},{6,30},{7,31},{8,16},{9,... | collective-permute-start | bytes 1228808 | tf_op jit(solution)/shard_map/ppermute | solution.py:439
  521.5 19.4 %collective-permute-start.30 = (bf16[80,5120]{1,0:T(8,128)(2,1)S(1)}, bf16[80,5120]{1,0:T(8,128)(2,1)S(1)}, u32[]{:S(2)}, u32[]{:S(2)}) collective-permute-start(bf16[80,5120]{1,0:T(8,128)(2,1)S(1)} %constant_dynamic-slice_fusion.14), channel_id=1, source_target_pairs={{0,24},{1,25},{2,26},{3,27},{4,28},{5,29},{6,30},{7,31},{8,16},{9,... | collective-permute-start | bytes 2457608 | tf_op jit(solution)/shard_map/ppermute | solution.py:439
  523.2 19.0 %collective-permute-start.26 = (bf16[80,5120]{1,0:T(8,128)(2,1)S(1)}, bf16[80,5120]{1,0:T(8,128)(2,1)S(1)}, u32[]{:S(2)}, u32[]{:S(2)}) collective-permute-start(bf16[80,5120]{1,0:T(8,128)(2,1)S(1)} %constant_dynamic-slice_fusion.18), channel_id=1, source_target_pairs={{0,6},{1,7},{2,4},{3,5},{4,2},{5,3},{6,0},{7,1},{8,14},{9,15},{10,... | collective-permute-start | bytes 2457608 | tf_op jit(solution)/shard_map/ppermute | solution.py:439
  530.6 22.1 %collective-permute-start.42 = (bf16[80,1280]{1,0:T(8,128)(2,1)S(1)}, bf16[80,1280]{1,0:T(8,128)(2,1)S(1)}, u32[]{:S(2)}, u32[]{:S(2)}) collective-permute-start(bf16[80,1280]{1,0:T(8,128)(2,1)S(1)} %constant_dynamic-slice_fusion.3), channel_id=1, source_target_pairs={{0,2},{1,3},{2,0},{3,1},{4,6},{5,7},{6,4},{7,5},{8,10},{9,11},{10,... | collective-permute-start | bytes 614408 | tf_op jit(solution)/shard_map/ppermute | solution.py:439
  532.3 20.5 %collective-permute-start.38 = (bf16[80,1280]{1,0:T(8,128)(2,1)S(1)}, bf16[80,1280]{1,0:T(8,128)(2,1)S(1)}, u32[]{:S(2)}, u32[]{:S(2)}) collective-permute-start(bf16[80,1280]{1,0:T(8,128)(2,1)S(1)} %constant_dynamic-slice_fusion.7), channel_id=1, source_target_pairs={{0,8},{1,9},{2,10},{3,11},{4,12},{5,13},{6,14},{7,15},{8,0},{9,1},... | collective-permute-start | bytes 614408 | tf_op jit(solution)/shard_map/ppermute | solution.py:439
  542.4 8.8 %collective-permute-start.27 = (bf16[40,5120]{1,0:T(8,128)(2,1)S(1)}, bf16[40,5120]{1,0:T(8,128)(2,1)S(1)}, u32[]{:S(2)}, u32[]{:S(2)}) collective-permute-start(bf16[40,5120]{1,0:T(8,128)(2,1)S(1)} %constant_dynamic-slice_fusion.17), channel_id=1, source_target_pairs={{0,8},{1,9},{2,10},{3,11},{4,12},{5,13},{6,14},{7,15},{8,0},{9,1},... | collective-permute-start | bytes 1228808 | tf_op jit(solution)/shard_map/ppermute | solution.py:439
  (53 other events, 353.0 us)
Sparse Core Ops, SparseCore 0:
  25.9 82.0 all-gather.2
